TPU v7x, 32 devices: a whole 2x2x4 slice. The times are simulated.
32 devices in a mesh: tile: 8 (over z, x), wp: 4 (over y, core).
Axes of the slice: x: 2, y: 2, z: 4, core: 2. Of those that a mesh axis runs over, the one named last changes fastest.
Arguments:
- visibilities: float32 [8192, 2, 128], P(('tile', 'wp')), may hold values from -6 to 6
- vis_weight: float32 [8192, 128], P(('tile', 'wp')), may hold values from 0.2 to 5
- cell_index: int32 [8192, 128], P(('tile', 'wp')), may hold values from 0 to 4095
- tap_offsets: int32 [8192, 128], P(('tile', 'wp')), may hold values from 0 to 255
- routes: int32 [8192, 1], P(('tile', 'wp')), may hold values from 0 to 31; in each aligned block of 256 rows (0 to 255, 256 to 511, ...) at most 16 rows name the same one
- patch_index: int32 [8192], P(('tile', 'wp')), may hold values from 0 to 255
- kernel: float32 [16, 8], replicated, may hold values from 0.1 to 1
Outputs:
- uv_grid: float32 [4, 8, 2, 1024, 1024], P('wp', 'tile')
Inputs may be any that keep to these rules, and one draw needn't show every extreme that they name: `routes`: the 256 blocks of one device name no value more than 16 times, a bound that some block reaches.
All inputs are finite; a program needn't handle non-finite values.
Results may differ from a plain program's by a relative error of at most 0.0003.
Values sent between devices are 32-bit elements; how exact they have to be, the bound alone decides.
No kernel may reach another device: no remote copies, remote signals or barrier semaphores. Data moves between devices by JAX's collectives and lax.ppermute only.
A program may use at most 192 MiB of HBM per device.

v0:
```python
import functools

import jax
import jax.numpy as jnp
from jax import lax
from jax.experimental import pallas as pl
from jax.experimental.pallas import tpu as pltpu
from jax.sharding import PartitionSpec as P

TCOLS = 8
SUB = 64
KW = 8
OVER = 16
TILE = 1024
ROWS = 128
SIDE = TILE // SUB
PATCHES = SIDE * SIDE
ROW_BLOCK = 2 * (SUB + KW)
FIRST = SIDE
DUMMY = FIRST + PATCHES
LONG, SHORT = 64, 16

f32 = jnp.float32
bf16 = jnp.bfloat16


def lanes(shape):
    return lax.broadcasted_iota(jnp.int32, shape, len(shape) - 1)


def pack_kernel(peers, cap, routes, patch, vis, weight, cell, tap, out, acc, *scratch):
    routes_s, patch_s, vis_v, weight_v, cell_v, tap_v, meta, meta_v, place, sems = scratch
    blocks = vis.shape[0]
    rows = 3 * cap + 1
    sources = (routes, patch, vis, weight, cell, tap)
    targets = (routes_s, patch_s, vis_v, weight_v, cell_v, tap_v)
    copies = [pltpu.make_async_copy(a, b, sems.at[i]) for i, (a, b) in enumerate(zip(sources, targets))]
    for copy in copies:
        copy.start()

    steps = blocks // 8
    me = lax.axis_index("half")

    def bucket_row(d):
        upper = jnp.where(d >= peers // 2, 1, 0)
        return ((d - upper * (peers // 2)) * 2 + (upper ^ me)) * rows

    early = acc.shape[0] - 6 * steps

    def clear_accumulators(first, number):
        for i in range(number):
            acc[first + i] = jnp.zeros((ROW_BLOCK, ROWS), f32)

    def clear(d, carry):
        meta[d, cap] = 0
        return carry

    def clear_one(i, carry):
        clear_accumulators(i, 1)
        return carry

    lax.fori_loop(0, peers, clear, 0, unroll=8)
    lax.fori_loop(0, early, clear_one, 0)
    copies[0].wait()
    copies[1].wait()

    def choose(step, carry):
        clear_accumulators(early + 4 * step, 4)
        for i in range(8):
            b = step * 8 + i
            d = routes_s[b]
            k = meta[d, cap]
            meta[d, cap] = k + 1
            meta[d, k] = patch_s[b]
            place[b] = bucket_row(d) + 3 * k
        return carry

    lax.fori_loop(0, steps, choose, 0)
    meta_copy = pltpu.make_async_copy(meta, meta_v, sems.at[6])
    meta_copy.start()
    for copy in copies[2:]:
        copy.wait()

    def move(step, carry):
        clear_accumulators(early + 4 * steps + 2 * step, 2)
        first = pl.multiple_of(step * 8, 8)
        block_rows = pl.ds(first, 8)
        w = weight_v[block_rows, :]
        c = cell_v[block_rows, :]
        t = tap_v[block_rows, :]
        at_u = ((t >> 4) << 3) | ((c >> 6) & 7)
        at_v = ((t & 15) << 3) | (c & 7)
        code = (((c >> 9) << 17) | (((c >> 3) & 7) << 14) | (at_u << 7) | at_v).astype(f32)
        for i in range(8):
            row = place[first + i]
            both = vis_v[first + i] * w[i : i + 1, :]
            out[row] = both[0:1, :]
            out[row + 1] = both[1:2, :]
            out[row + 2] = code[i : i + 1, :]
        return carry

    lax.fori_loop(0, steps, move, 0)
    meta_copy.wait()

    def put_meta(d, carry):
        out[bucket_row(d) + 3 * cap] = meta_v[pl.ds(d, 1), :].astype(f32)
        return carry

    lax.fori_loop(0, peers, put_meta, 0, unroll=8)


def split(x):
    hi = x.astype(bf16)
    return hi, (x - hi.astype(f32)).astype(bf16)


def twice(x):
    return jnp.concatenate([x, x], axis=0)


def look_up(table, index):
    numbers = lax.GatherDimensionNumbers(
        offset_dims=(),
        collapsed_slice_dims=(1,),
        start_index_map=(1,),
        operand_batching_dims=(0,),
        start_indices_batching_dims=(0,),
    )
    return lax.gather(
        table, index[..., None], numbers, (1, 1), mode=lax.GatherScatterMode.PROMISE_IN_BOUNDS
    )


def spread(picks, values):
    zero = jnp.zeros((16, ROWS), bf16)
    return [[jnp.where(pick, value, zero) for pick in picks] for value in values]


def patch_product(re, im, code, parity, table):
    sub = lax.broadcasted_iota(jnp.int32, (8, ROWS), 0)
    at_v = code & 127
    at_u = (code >> 7) & 127
    ku = look_up(table, at_u)
    kv = look_up(table, at_v)
    group_u = ((code >> 17) & 7) + jnp.where(sub < (at_u & 7), 1, 0)
    group_v = ((code >> 14) & 7) + jnp.where(sub < (at_v & 7), 1, 0) + 8 * parity
    step_u = twice(group_u.astype(f32)).astype(bf16)
    step_v = jnp.concatenate([group_v & 15, (group_v + 15) & 15], axis=0).astype(f32).astype(bf16)

    u_hi, u_lo = split(jnp.concatenate([re * ku, im * ku], axis=0))
    hi_rows, lo_rows = spread([step_u == float(g) for g in range(SUB // 8 + 1)], [u_hi, u_lo])
    left_hi, left_lo = jnp.concatenate(hi_rows, axis=0), jnp.concatenate(lo_rows, axis=0)
    left = jnp.concatenate([left_hi, left_lo, left_hi], axis=1)

    v_hi, v_lo = split(twice(kv))
    hi_rows, lo_rows = spread([step_v == 2.0 * g for g in range(ROWS // 16)], [v_hi, v_lo])
    right_hi, right_lo = jnp.concatenate(hi_rows, axis=0), jnp.concatenate(lo_rows, axis=0)
    right = jnp.concatenate([right_hi, right_hi, right_lo], axis=1)
    return lax.dot_general(left, right, (((1,), (1,)), ((), ())), preferred_element_type=f32)


def tap_table(kernel):
    sub = lax.broadcasted_iota(jnp.int32, (8, ROWS), 0)
    lane = lanes((8, ROWS))
    which_tap = (sub - lane) & 7
    which_level = lane >> 3
    table = jnp.zeros((8, ROWS), f32)
    for a in range(KW):
        row = jnp.zeros((8, ROWS), f32)
        for o in range(OVER):
            row = jnp.where(which_level == o, kernel[a, o], row)
        table = jnp.where(which_tap == a, row, table)
    return table


def add_kernel(sources, cap, stride, with_edge, kernel, arrived, acc_in, acc, *scratch):
    right, scratch = (scratch[0], scratch[1:]) if with_edge else (None, scratch)
    meta_v, meta, slots, kernel_s, meta_sem, kernel_sem = scratch
    kernel_copy = pltpu.make_async_copy(kernel, kernel_s, kernel_sem)
    kernel_copy.start()
    lane_row = lanes((1, ROWS))

    def entries(s, carry):
        row = arrived[s * stride + 3 * cap].astype(jnp.int32)
        entry = (s * stride + 3 * lane_row) * 512 + (row + FIRST)
        meta_v[pl.ds(s, 1), :] = jnp.where(lane_row < cap, entry, row)
        return carry

    lax.fori_loop(0, sources, entries, 0, unroll=8)
    meta_copy = pltpu.make_async_copy(meta_v, meta, meta_sem)
    meta_copy.start()
    kernel_copy.wait()
    table = tap_table(kernel_s)
    meta_copy.wait()

    def gather_source(s, total):
        for k in range(cap):
            slots[total + k] = meta[s, k]
        return total + meta[s, cap]

    total = lax.fori_loop(0, sources, gather_source, 0, unroll=2)
    for k in range(SHORT):
        slots[total + k] = DUMMY

    def add(first, number):
        for i in range(number):
            entry = slots[first + i]
            row = entry >> 9
            where_to = entry & 511
            re = jnp.broadcast_to(arrived[row], (8, ROWS))
            im = jnp.broadcast_to(arrived[row + 1], (8, ROWS))
            code = jnp.broadcast_to(arrived[row + 2], (8, ROWS)).astype(jnp.int32)
            acc[where_to] += patch_product(re, im, code, entry & 1, table)

    def long_step(step, carry):
        add(step * LONG, LONG)
        return carry

    long_steps = total // LONG
    lax.fori_loop(0, long_steps, long_step, 0)
    done = long_steps * LONG

    def short_step(step, carry):
        add(done + step * SHORT, SHORT)
        return carry

    lax.fori_loop(0, (total - done + SHORT - 1) // SHORT, short_step, 0)

    if not with_edge:
        return

    lane = lanes((8, ROWS))

    def pack_edge(pair, carry):
        for c in range(2):
            edge = jnp.zeros((8, ROWS), f32)
            for k in range(16):
                last = rows_of(acc, c, k % 8, pair * 2 + k // 8, SIDE - 1)
                moved = pltpu.roll(last, 8 * k, 1) if k else last
                edge = jnp.where((lane >> 3) == k, moved, edge)
            right[c, pair] = edge
        return carry

    lax.fori_loop(0, SIDE // 2, pack_edge, 0)


def rows_of(acc, c, h, band, col):
    part = acc[FIRST + band * SIDE + col, pl.ds(16 * h + 8 * c, 8), :]
    if h == 0:
        part = part + acc[band * SIDE + col, pl.ds(2 * SUB + 8 * c, 8), :]
    return part


def fold_kernel(with_low, acc, out, first, *rest):
    low, rest = (rest[0], rest[1:]) if with_low else (None, rest)
    stage, out_sems = rest
    lane = lanes((8, ROWS))

    def copy_out(band):
        rows = pl.ds(band * SUB, SUB)
        return pltpu.make_async_copy(
            stage.at[:, rows, :], out.at[:, rows, pl.ds(ROWS, TILE - ROWS)], out_sems.at[band]
        )

    def fold(band, carry):
        for c in range(2):
            for h in range(8):
                before = jnp.zeros((8, ROWS), f32)
                for t in range(TILE // ROWS):
                    even = rows_of(acc, c, h, band, 2 * t)
                    odd = rows_of(acc, c, h, band, 2 * t + 1)
                    rows = pl.ds(band * SUB + 8 * h, 8)
                    columns = even + jnp.where(lane < SUB, before, odd)
                    if t == 0:
                        first[c, rows, :] = columns
                    else:
                        stage[c, rows, pl.ds((t - 1) * ROWS, ROWS)] = columns
                    before = odd
        copy_out(band).start()
        return carry

    lax.fori_loop(0, SIDE, fold, 0)
    if with_low:
        for c in range(2):
            before = jnp.zeros((8, ROWS), f32)
            for t in range(TILE // ROWS):
                rows = pl.ds(2 * SUB + 8 * c, 8)
                even = acc[FIRST + (SIDE - 1) * SIDE + 2 * t, rows, :]
                odd = acc[FIRST + (SIDE - 1) * SIDE + 2 * t + 1, rows, :]
                low[c, :, pl.ds(t * ROWS, ROWS)] = even + jnp.where(lane < SUB, before, odd)
                before = odd
            low[c, :, pl.ds(TILE, ROWS)] = jnp.where(lane < KW, before, 0.0)

    def finish(band, carry):
        copy_out(band).wait()
        return carry

    lax.fori_loop(0, SIDE, finish, 0)


def edge_kernel(edge, first, grid_in, grid_out, columns, out_sems):
    lane = lanes((8, ROWS))
    pairs = SIDE // 2

    def put(pair):
        rows = pl.ds(pair * 2 * SUB, 2 * SUB)
        return pltpu.make_async_copy(
            columns.at[:, rows, :], grid_out.at[:, rows, pl.ds(0, ROWS)], out_sems.at[pair]
        )

    def add(pair, carry):
        for c in range(2):
            packed = edge[c, pair]
            for k in range(16):
                moved = pltpu.roll(packed, ROWS - 8 * k, 1) if k else packed
                rows = pl.ds(pair * 2 * SUB + 8 * k, 8)
                columns[c, rows, :] = first[c, rows, :] + jnp.where(lane < KW, moved, 0.0)
        put(pair).start()
        return carry

    lax.fori_loop(0, pairs, add, 0)
    for pair in range(pairs):
        put(pair).wait()


def in_hbm(x):
    return pltpu.with_memory_space_constraint(x, pltpu.HBM)


def shifted(block, distance):
    tiles = ("half", "tile")
    devices = range(lax.axis_size(tiles))
    route = [(i - distance, i) for i in devices if i - distance in devices]
    return lax.ppermute(block, tiles, route)


def shards(visibilities, vis_weight, cell_index, tap_offsets, routes, patch_index, kernel):
    blocks = visibilities.shape[0]
    tile_count = lax.axis_size(("half", "tile"))
    plane_count = lax.axis_size("wp")
    peers = tile_count * plane_count
    cap = max(2, 2 * blocks // peers)
    rows = 3 * cap + 1
    vmem = pl.BlockSpec(memory_space=pltpu.VMEM)
    hbm = pl.BlockSpec(memory_space=pltpu.HBM)

    acc_shape = (max(DUMMY + 1, 6 * (blocks // 8)), ROW_BLOCK, ROWS)

    buckets, acc = pl.pallas_call(
        functools.partial(pack_kernel, peers, cap),
        out_shape=[jax.ShapeDtypeStruct((peers * rows, 1, ROWS), f32), pltpu.VMEM(acc_shape, f32)],
        in_specs=[hbm] * 6,
        out_specs=[vmem, vmem],
        scratch_shapes=[
            pltpu.SMEM((blocks,), jnp.int32),
            pltpu.SMEM((blocks,), jnp.int32),
            pltpu.VMEM((blocks, 2, ROWS), f32),
            pltpu.VMEM((blocks, ROWS), f32),
            pltpu.VMEM((blocks, ROWS), jnp.int32),
            pltpu.VMEM((blocks, ROWS), jnp.int32),
            pltpu.SMEM((peers, ROWS), jnp.int32),
            pltpu.VMEM((peers, ROWS), jnp.int32),
            pltpu.SMEM((blocks,), jnp.int32),
            pltpu.SemaphoreType.DMA((7,)),
        ],
        compiler_params=pltpu.CompilerParams(vmem_limit_bytes=8 << 20),
        name="pack",
    )(*[in_hbm(x) for x in (routes[:, 0], patch_index, visibilities, vis_weight, cell_index, tap_offsets)])

    arrived = lax.all_to_all(buckets, ("tile", "wp"), split_axis=0, concat_axis=0, tiled=True)

    sources = peers // 2
    far = arrived.reshape(sources, 2 * rows, 1, ROWS)[:, rows:].reshape(sources * rows, 1, ROWS)
    far = lax.ppermute(far, "half", [(0, 1), (1, 0)])

    def add(part, stride, acc, with_edge):
        out_shape, out_specs = [pltpu.VMEM(acc_shape, f32)], [vmem]
        if with_edge:
            out_shape.append(jax.ShapeDtypeStruct((2, SIDE // 2, 8, ROWS), f32))
            out_specs.append(vmem)
        return pl.pallas_call(
            functools.partial(add_kernel, sources, cap, stride, with_edge),
            out_shape=out_shape,
            in_specs=[hbm, vmem, vmem],
            out_specs=out_specs,
            scratch_shapes=[
                pltpu.VMEM((sources, ROWS), jnp.int32),
                pltpu.SMEM((sources, ROWS), jnp.int32),
                pltpu.SMEM((sources * cap + max(cap, SHORT),), jnp.int32),
                pltpu.SMEM((KW, OVER), f32),
                pltpu.SemaphoreType.DMA,
                pltpu.SemaphoreType.DMA,
            ],
            input_output_aliases={2: 0},
            compiler_params=pltpu.CompilerParams(vmem_limit_bytes=4 << 20),
            cost_estimate=pl.CostEstimate(flops=1 << 33, bytes_accessed=1 << 20, transcendentals=0),
            name="add_far" if with_edge else "add_near",
        )(in_hbm(kernel.T), part, acc)

    (acc,) = add(arrived, 2 * rows, acc, False)
    acc, right = add(far, rows, acc, True)

    place = lax.axis_index(("half", "tile"))
    from_left = shifted(right, 1)

    with_low = tile_count > TCOLS
    out_shape = [jax.ShapeDtypeStruct((2, TILE, TILE), f32), jax.ShapeDtypeStruct((2, TILE, ROWS), f32)]
    out_specs = [hbm, vmem]
    if with_low:
        out_shape.append(jax.ShapeDtypeStruct((2, KW, TILE + ROWS), f32))
        out_specs.append(vmem)
    own, first, *low = pl.pallas_call(
        functools.partial(fold_kernel, with_low),
        out_shape=out_shape,
        in_specs=[vmem],
        out_specs=out_specs,
        scratch_shapes=[pltpu.VMEM((2, TILE, TILE - ROWS), f32), pltpu.SemaphoreType.DMA((SIDE,))],
        compiler_params=pltpu.CompilerParams(vmem_limit_bytes=12 << 20),
        cost_estimate=pl.CostEstimate(flops=1 << 22, bytes_accessed=16 << 20, transcendentals=0),
        name="fold",
    )(acc)

    if with_low:
        from_left = jnp.where(place % TCOLS == 0, 0.0, from_left)
    own = pl.pallas_call(
        edge_kernel,
        out_shape=jax.ShapeDtypeStruct((2, TILE, TILE), f32),
        in_specs=[vmem, vmem, hbm],
        out_specs=hbm,
        scratch_shapes=[
            pltpu.VMEM((2, TILE, ROWS), f32),
            pltpu.SemaphoreType.DMA((SIDE // 2,)),
        ],
        input_output_aliases={2: 0},
        compiler_params=pltpu.CompilerParams(vmem_limit_bytes=4 << 20),
        name="edges",
    )(from_left, first, own)
    if with_low:
        (low,) = low
        from_above = shifted(low, TCOLS)
        from_corner = shifted(low[:, :, TILE:], TCOLS + 1)
        from_corner = jnp.where(place % TCOLS == 0, 0.0, from_corner)
        own = own.at[:, :KW, :].add(from_above[:, :, :TILE])
        own = own.at[:, :KW, :ROWS].add(from_corner)
    return own.reshape(1, 1, 2, TILE, TILE)


def solution(mesh):
    tiles, planes = mesh.shape["tile"], mesh.shape["wp"]
    halves = jax.sharding.Mesh(mesh.devices.reshape(2, tiles // 2, planes), ("half", "tile", "wp"))
    every = ("half", "tile", "wp")
    in_specs = (
        P(every, None, None),
        P(every, None),
        P(every, None),
        P(every, None),
        P(every, None),
        P(every),
        P(),
    )
    out_specs = P("wp", ("half", "tile"), None, None, None)
    return jax.shard_map(shards, mesh=halves, in_specs=in_specs, out_specs=out_specs, check_vma=False)
```

profile of v0, /device:TPU:1, one launch (start us, length us, event | category | flops | bytes accessed | tf_op | source)
XLA Modules:
  0.0 63.4 jit_solution(754549539686382133)
XLA Ops:
  0.0 4.2 %pack.1 = (f32[1568,1,128]{2,1,0:T(1,128)S(1)}, f32[273,144,128]{2,1,0:T(8,128)S(1)}) custom-call(s32[256]{0:T(256)} %bitcast.9, s32[256]{0:T(256)} %patch.1, f32[256,2,128]{2,1,0:T(2,128)} %vis.1, f32[256,128]{1,0:T(8,128)} %weight.1, s32[256,128]{1,0:T(8,128)} %cell.1, s32[256,128]{1,0:T(8,128)} %tap.1), custom_call_target="tpu_custom_call" | custom-call | tf_op jit(solution)/shard_map/pack/pallas_call | solution.py:349
  4.3 18.5 %all_to_all.5.arrived = f32[1568,1,128]{2,1,0:T(1,128)S(1)} all-to-all(f32[1568,1,128]{2,1,0:T(1,128)S(1)} %get-tuple-element.11), channel_id=1, replica_groups=mesh['half'=2,'tile'=4,'wp'=4] {'tile','wp'}, dimensions={0} | all-to-all | bytes 1605632 | tf_op jit(solution)/shard_map/all_to_all | solution.py:370
  22.8 2.4 %collective-permute-start = (f32[784,1,128]{2,1,0:T(1,128)S(1)}, f32[784,1,128]{2,1,0:T(1,128)S(1)}, u32[]{:S(2)}, u32[]{:S(2)}) collective-permute-start(f32[784,1,128]{2,1,0:T(1,128)S(1)} %bitcast.6), channel_id=1, source_target_pairs={{0,16},{16,0},{1,17},{17,1},{2,18},{18,2},{3,19},{19,3},{4,20},{20... | collective-permute-start | bytes 1204232 | tf_op jit(solution)/shard_map/ppermute | solution.py:374
  25.2 7.3 %add_near.1.acc_in = f32[273,144,128]{2,1,0:T(8,128)S(1)} custom-call(f32[8,16]{1,0:T(8,128)} %bitcast.7, f32[1568,1,128]{2,1,0:T(1,128)S(1)} %all_to_all.5.arrived, f32[273,144,128]{2,1,0:T(8,128)S(1)} %get-tuple-element.12.acc_in), custom_call_target="tpu_custom_call", output_to_operand_aliasing={{}: (2, {})} | custom-call | flops 8589934592 | bytes 1048576 | tf_op jit(solution)/shard_map/add_near/pallas_call | solution.py:381
  32.5 10.6 %collective-permute-done.arrived = f32[784,1,128]{2,1,0:T(1,128)S(1)} collective-permute-done((f32[784,1,128]{2,1,0:T(1,128)S(1)}, f32[784,1,128]{2,1,0:T(1,128)S(1)}, u32[]{:S(2)}, u32[]{:S(2)}) %collective-permute-start) | collective-permute-done | bytes 401440 | tf_op jit(solution)/shard_map/ppermute | solution.py:374
  43.1 7.4 %add_far.1 = (f32[273,144,128]{2,1,0:T(8,128)S(1)}, f32[2,8,8,128]{3,2,1,0:T(8,128)S(1)}) custom-call(f32[8,16]{1,0:T(8,128)} %bitcast.8, f32[784,1,128]{2,1,0:T(1,128)S(1)} %collective-permute-done.arrived, f32[273,144,128]{2,1,0:T(8,128)S(1)} %add_near.1.acc_in), custom_call_target="tpu_custom_call", output_to_operand_aliasing={{0}: (2, {})} | custom-call | flops 8589934592 | bytes 1048576 | tf_op jit(solution)/shard_map/add_far/pallas_call | solution.py:381
  50.5 8.2 %collective-permute-start.1 = (f32[2,8,8,128]{3,2,1,0:T(8,128)S(1)}, f32[2,8,8,128]{3,2,1,0:T(8,128)S(1)}, u32[]{:S(2)}, u32[]{:S(2)}) collective-permute-start(f32[2,8,8,128]{3,2,1,0:T(8,128)S(1)} %get-tuple-element.13), channel_id=1, source_target_pairs={{0,4},{4,8},{8,12},{12,16},{16,20},{20,24},{24,28},{1,5},{5,9},{9,... | collective-permute-start | bytes 196616 | tf_op jit(solution)/shard_map/ppermute | solution.py:334
  58.7 3.2 %fold.1 = (f32[2,1024,1024]{2,1,0:T(8,128)}, f32[2,1024,128]{2,1,0:T(8,128)S(1)}) custom-call(f32[273,144,128]{2,1,0:T(8,128)S(1)} %get-tuple-element.14.acc), custom_call_target="tpu_custom_call" | custom-call | flops 4194304 | bytes 16777216 | tf_op jit(solution)/shard_map/fold/pallas_call | solution.py:412
  61.9 0.0 collective-permute-done.1.edge
  61.9 1.5 %edges.1 = f32[2,1024,1024]{2,1,0:T(8,128)} custom-call(f32[2,8,8,128]{3,2,1,0:T(8,128)S(1)} %collective-permute-done.1.edge, f32[2,1024,128]{2,1,0:T(8,128)S(1)} %get-tuple-element.15.first, f32[2,1024,1024]{2,1,0:T(8,128)} %get-tuple-element.16.grid_in), custom_call_target="tpu_custom_call", output_to_operand_aliasing={{}: (2, {})} | custom-call | tf_op jit(solution)/shard_map/edges/pallas_call | solution.py:425
  (1 shorter events, 0.0 us)
Async XLA Ops:
  22.8 20.3 %collective-permute-start = (f32[784,1,128]{2,1,0:T(1,128)S(1)}, f32[784,1,128]{2,1,0:T(1,128)S(1)}, u32[]{:S(2)}, u32[]{:S(2)}) collective-permute-start(f32[784,1,128]{2,1,0:T(1,128)S(1)} %bitcast.6), channel_id=1, source_target_pairs={{0,16},{16,0},{1,17},{17,1},{2,18},{18,2},{3,19},{19,3},{4,20},{20... | collective-permute-start | bytes 1204232 | tf_op jit(solution)/shard_map/ppermute | solution.py:374
  50.5 11.4 %collective-permute-start.1 = (f32[2,8,8,128]{3,2,1,0:T(8,128)S(1)}, f32[2,8,8,128]{3,2,1,0:T(8,128)S(1)}, u32[]{:S(2)}, u32[]{:S(2)}) collective-permute-start(f32[2,8,8,128]{3,2,1,0:T(8,128)S(1)} %get-tuple-element.13), channel_id=1, source_target_pairs={{0,4},{4,8},{8,12},{12,16},{16,20},{20,24},{24,28},{1,5},{5,9},{9,... | collective-permute-start | bytes 196616 | tf_op jit(solution)/shard_map/ppermute | solution.py:334
where the time goes:
time: 63.6 us; the launch traced here: 63.4 us
  Pallas kernels  23.6 us (37%)
  blocking collectives  18.5 us (29%)
  waiting for transfers between devices  10.6 us (17%)
  starting transfers between devices  10.5 us (17%)
    all_to_all x1, blocking collectives, shards(): lax.all_to_all(buckets, ('tile', 'wp'), split_axis=0, concat_axis=0, tile...  18.5 us
    pallas_call x2, Pallas kernels, add(): pl.pallas_call(functools.partial(add_kernel, sources, cap, stride, with_e...  14.7 us
    ppermute x1, waiting for transfers between devices, shards(): far = lax.ppermute(far, 'half', [(0, 1), (1, 0)])  10.6 us
    ppermute x1, starting transfers between devices, shifted(): return lax.ppermute(block, tiles, route)  8.17 us
    pallas_call x1, Pallas kernels, shards(): pl.pallas_call(functools.partial(pack_kernel, peers, cap), out_shape=[jax...  4.25 us
    pallas_call x1, Pallas kernels, shards(): pl.pallas_call(functools.partial(fold_kernel, with_low), out_shape=out_sh...  3.18 us
    ppermute x1, starting transfers between devices, shards(): far = lax.ppermute(far, 'half', [(0, 1), (1, 0)])  2.37 us
    pallas_call x1, Pallas kernels, shards(): pl.pallas_call(edge_kernel, out_shape=jax.ShapeDtypeStruct((2, TILE, TILE...  1.54 us
  transfers between devices with their start and end apart: 2, of which 1 were waited for; matrix products, arithmetic and copies ran while one was open for 0% of the time, Pallas kernels for 17%

commit v1 on v0

--- a/solution.py
+++ b/solution.py
@@ -29,7 +29,7 @@
 
 
 def pack_kernel(peers, cap, routes, patch, vis, weight, cell, tap, out, acc, *scratch):
-    routes_s, patch_s, vis_v, weight_v, cell_v, tap_v, meta, meta_v, place, sems = scratch
+    routes_s, patch_s, vis_v, weight_v, cell_v, tap_v, meta, meta_v, place, bases, sems = scratch
     blocks = vis.shape[0]
     rows = 3 * cap + 1
     sources = (routes, patch, vis, weight, cell, tap)
@@ -41,10 +41,6 @@
     steps = blocks // 8
     me = lax.axis_index("half")
 
-    def bucket_row(d):
-        upper = jnp.where(d >= peers // 2, 1, 0)
-        return ((d - upper * (peers // 2)) * 2 + (upper ^ me)) * rows
-
     early = acc.shape[0] - 6 * steps
 
     def clear_accumulators(first, number):
@@ -53,6 +49,8 @@
 
     def clear(d, carry):
         meta[d, cap] = 0
+        upper = jnp.where(d >= peers // 2, 1, 0)
+        bases[d] = ((d - upper * (peers // 2)) * 2 + (upper ^ me)) * rows
         return carry
 
     def clear_one(i, carry):
@@ -72,7 +70,7 @@
             k = meta[d, cap]
             meta[d, cap] = k + 1
             meta[d, k] = patch_s[b]
-            place[b] = bucket_row(d) + 3 * k
+            place[b] = bases[d] + 3 * k
         return carry
 
     lax.fori_loop(0, steps, choose, 0)
@@ -103,7 +101,7 @@
     meta_copy.wait()
 
     def put_meta(d, carry):
-        out[bucket_row(d) + 3 * cap] = meta_v[pl.ds(d, 1), :].astype(f32)
+        out[bases[d] + 3 * cap] = meta_v[pl.ds(d, 1), :].astype(f32)
         return carry
 
     lax.fori_loop(0, peers, put_meta, 0, unroll=8)
@@ -173,9 +171,21 @@
     return table
 
 
-def add_kernel(sources, cap, stride, with_edge, kernel, arrived, acc_in, acc, *scratch):
+def add_kernel(sources, cap, stride, passed, with_edge, kernel, arrived, acc_in, acc, *scratch):
     right, scratch = (scratch[0], scratch[1:]) if with_edge else (None, scratch)
-    meta_v, meta, slots, kernel_s, meta_sem, kernel_sem = scratch
+    handed, scratch = (scratch[0], scratch[1:]) if passed else (None, scratch)
+    meta_v, meta, slots, kernel_s, meta_sem, kernel_sem, *handed_sem = scratch
+    half = stride // 2
+    handed_copies = [
+        pltpu.make_async_copy(
+            arrived.at[pl.ds((sources - passed + i) * stride + half, half)],
+            handed.at[pl.ds(i * half, half)],
+            handed_sem[0].at[i],
+        )
+        for i in range(passed)
+    ]
+    for copy in handed_copies:
+        copy.start()
     kernel_copy = pltpu.make_async_copy(kernel, kernel_s, kernel_sem)
     kernel_copy.start()
     lane_row = lanes((1, ROWS))
@@ -226,6 +236,8 @@
 
     lax.fori_loop(0, (total - done + SHORT - 1) // SHORT, short_step, 0)
 
+    for copy in handed_copies:
+        copy.wait()
     if not with_edge:
         return
 
@@ -361,6 +373,7 @@
             pltpu.SMEM((peers, ROWS), jnp.int32),
             pltpu.VMEM((peers, ROWS), jnp.int32),
             pltpu.SMEM((blocks,), jnp.int32),
+            pltpu.SMEM((peers,), jnp.int32),
             pltpu.SemaphoreType.DMA((7,)),
         ],
         compiler_params=pltpu.CompilerParams(vmem_limit_bytes=8 << 20),
@@ -370,16 +383,21 @@
     arrived = lax.all_to_all(buckets, ("tile", "wp"), split_axis=0, concat_axis=0, tiled=True)
 
     sources = peers // 2
-    far = arrived.reshape(sources, 2 * rows, 1, ROWS)[:, rows:].reshape(sources * rows, 1, ROWS)
-    far = lax.ppermute(far, "half", [(0, 1), (1, 0)])
-
-    def add(part, stride, acc, with_edge):
+    later = sources // 4
+    across = [(0, 1), (1, 0)]
+    far = arrived.reshape(sources, 2 * rows, 1, ROWS)[: sources - later, rows:]
+    far = lax.ppermute(far.reshape((sources - later) * rows, 1, ROWS), "half", across)
+
+    def add(name, part, sources, stride, acc, passed=0, with_edge=False):
         out_shape, out_specs = [pltpu.VMEM(acc_shape, f32)], [vmem]
         if with_edge:
             out_shape.append(jax.ShapeDtypeStruct((2, SIDE // 2, 8, ROWS), f32))
             out_specs.append(vmem)
+        if passed:
+            out_shape.append(jax.ShapeDtypeStruct((passed * rows, 1, ROWS), f32))
+            out_specs.append(vmem)
         return pl.pallas_call(
-            functools.partial(add_kernel, sources, cap, stride, with_edge),
+            functools.partial(add_kernel, sources, cap, stride, passed, with_edge),
             out_shape=out_shape,
             in_specs=[hbm, vmem, vmem],
             out_specs=out_specs,
@@ -390,15 +408,18 @@
                 pltpu.SMEM((KW, OVER), f32),
                 pltpu.SemaphoreType.DMA,
                 pltpu.SemaphoreType.DMA,
+                *([pltpu.SemaphoreType.DMA((passed,))] if passed else []),
             ],
             input_output_aliases={2: 0},
             compiler_params=pltpu.CompilerParams(vmem_limit_bytes=4 << 20),
             cost_estimate=pl.CostEstimate(flops=1 << 33, bytes_accessed=1 << 20, transcendentals=0),
-            name="add_far" if with_edge else "add_near",
+            name=name,
         )(in_hbm(kernel.T), part, acc)
 
-    (acc,) = add(arrived, 2 * rows, acc, False)
-    acc, right = add(far, rows, acc, True)
+    acc, last = add("add_near", arrived, sources, 2 * rows, acc, passed=later)
+    last = lax.ppermute(last, "half", across)
+    (acc,) = add("add_far", far, sources - later, rows, acc)
+    acc, right = add("add_last", last, later, rows, acc, with_edge=True)
 
     place = lax.axis_index(("half", "tile"))
     from_left = shifted(right, 1)

time: 63.6 us -> 62.1 us (0.976)
  the two profiles are of different devices: /device:TPU:1 before, /device:TPU:0 now
where the time goes in v1:
time: 62.1 us; the launch traced here: 61.9 us
  Pallas kernels  36.3 us (58%)
  blocking collectives  19.6 us (32%)
  starting transfers between devices  4.02 us (6%)
  waiting for transfers between devices  1.84 us (3%)
    pallas_call x3, Pallas kernels, add(): pl.pallas_call(functools.partial(add_kernel, sources, cap, stride, passed...  27.9 us
    all_to_all x1, blocking collectives, shards(): lax.all_to_all(buckets, ('tile', 'wp'), split_axis=0, concat_axis=0, tile...  19.6 us
    pallas_call x1, Pallas kernels, shards(): pl.pallas_call(functools.partial(pack_kernel, peers, cap), out_shape=[jax...  3.64 us
    pallas_call x1, Pallas kernels, shards(): pl.pallas_call(functools.partial(fold_kernel, with_low), out_shape=out_sh...  3.18 us
    ppermute x1, starting transfers between devices, shards(): lax.ppermute(far.reshape((sources - later) * rows, 1, ROWS), 'half', across)  2.65 us
    ppermute x1, waiting for transfers between devices, shards(): lax.ppermute(far.reshape((sources - later) * rows, 1, ROWS), 'half', across)  1.83 us
    pallas_call x1, Pallas kernels, shards(): pl.pallas_call(edge_kernel, out_shape=jax.ShapeDtypeStruct((2, TILE, TILE...  1.54 us
    ppermute x1, starting transfers between devices, shifted(): return lax.ppermute(block, tiles, route)  1.29 us
  transfers between devices with their start and end apart: 3, of which 1 were waited for; matrix products, arithmetic and copies ran while one was open for 0% of the time, Pallas kernels for 42%

profile of v1, /device:TPU:0, one launch (start us, length us, event | category | flops | bytes accessed | tf_op | source)
XLA Modules:
  0.0 61.9 jit_solution(14020635858846813098)
XLA Ops:
  0.0 3.6 %pack.1 = (f32[1568,1,128]{2,1,0:T(1,128)S(1)}, f32[273,144,128]{2,1,0:T(8,128)S(1)}) custom-call(s32[256]{0:T(256)} %bitcast.10, s32[256]{0:T(256)} %patch.1, f32[256,2,128]{2,1,0:T(2,128)} %vis.1, f32[256,128]{1,0:T(8,128)} %weight.1, s32[256,128]{1,0:T(8,128)} %cell.1, s32[256,128]{1,0:T(8,128)} %tap.1), custom_call_target="tpu_custom_call" | custom-call | tf_op jit(solution)/shard_map/pack/pallas_call | solution.py:361
  3.6 19.6 %all_to_all.5.arrived = f32[1568,1,128]{2,1,0:T(1,128)S(1)} all-to-all(f32[1568,1,128]{2,1,0:T(1,128)S(1)} %get-tuple-element.13), channel_id=1, replica_groups=mesh['half'=2,'tile'=4,'wp'=4] {'tile','wp'}, dimensions={0} | all-to-all | bytes 1605632 | tf_op jit(solution)/shard_map/all_to_all | solution.py:383
  23.3 2.7 %collective-permute-start.1 = (f32[588,1,128]{2,1,0:T(1,128)S(1)}, f32[588,1,128]{2,1,0:T(1,128)S(1)}, u32[]{:S(2)}, u32[]{:S(2)}) collective-permute-start(f32[588,1,128]{2,1,0:T(1,128)S(1)} %bitcast.6), channel_id=1, source_target_pairs={{0,16},{16,0},{1,17},{17,1},{2,18},{18,2},{3,19},{19,3},{4,20},{20... | collective-permute-start | bytes 903176 | tf_op jit(solution)/shard_map/ppermute | solution.py:389
  25.9 12.9 %add_near.1 = (f32[273,144,128]{2,1,0:T(8,128)S(1)}, f32[196,1,128]{2,1,0:T(1,128)S(1)}) custom-call(f32[8,16]{1,0:T(8,128)} %bitcast.7, f32[1568,1,128]{2,1,0:T(1,128)S(1)} %all_to_all.5.arrived, f32[273,144,128]{2,1,0:T(8,128)S(1)} %get-tuple-element.14.acc_in), custom_call_target="tpu_custom_call", output_to_operand_aliasing={{0}: (2, {})} | custom-call | flops 8589934592 | bytes 1048576 | tf_op jit(solution)/shard_map/add_near/pallas_call | solution.py:399
  38.8 0.1 collective-permute-start
  38.9 1.8 %collective-permute-done.1.arrived = f32[588,1,128]{2,1,0:T(1,128)S(1)} collective-permute-done((f32[588,1,128]{2,1,0:T(1,128)S(1)}, f32[588,1,128]{2,1,0:T(1,128)S(1)}, u32[]{:S(2)}, u32[]{:S(2)}) %collective-permute-start.1) | collective-permute-done | bytes 301088 | tf_op jit(solution)/shard_map/ppermute | solution.py:389
  40.7 9.9 %add_far.1.acc_in = f32[273,144,128]{2,1,0:T(8,128)S(1)} custom-call(f32[8,16]{1,0:T(8,128)} %bitcast.8, f32[588,1,128]{2,1,0:T(1,128)S(1)} %collective-permute-done.1.arrived, f32[273,144,128]{2,1,0:T(8,128)S(1)} %get-tuple-element.16.acc_in), custom_call_target="tpu_custom_call", output_to_operand_aliasing={{}: (2, {})} | custom-call | flops 8589934592 | bytes 1048576 | tf_op jit(solution)/shard_map/add_far/pallas_call | solution.py:399
  50.7 0.0 collective-permute-done.arrived
  50.7 5.2 %add_last.1 = (f32[273,144,128]{2,1,0:T(8,128)S(1)}, f32[2,8,8,128]{3,2,1,0:T(8,128)S(1)}) custom-call(f32[8,16]{1,0:T(8,128)} %bitcast.9, f32[196,1,128]{2,1,0:T(1,128)S(1)} %collective-permute-done.arrived, f32[273,144,128]{2,1,0:T(8,128)S(1)} %add_far.1.acc_in), custom_call_target="tpu_custom_call", output_to_operand_aliasing={{0}: (2, {})} | custom-call | flops 8589934592 | bytes 1048576 | tf_op jit(solution)/shard_map/add_last/pallas_call | solution.py:399
  55.8 1.3 %collective-permute-start.2 = (f32[2,8,8,128]{3,2,1,0:T(8,128)S(1)}, f32[2,8,8,128]{3,2,1,0:T(8,128)S(1)}, u32[]{:S(2)}, u32[]{:S(2)}) collective-permute-start(f32[2,8,8,128]{3,2,1,0:T(8,128)S(1)} %get-tuple-element.17), channel_id=1, source_target_pairs={{0,4},{4,8},{8,12},{12,16},{16,20},{20,24},{24,28},{1,5},{5,9},{9,... | collective-permute-start | bytes 196616 | tf_op jit(solution)/shard_map/ppermute | solution.py:346
  57.1 3.2 %fold.1 = (f32[2,1024,1024]{2,1,0:T(8,128)}, f32[2,1024,128]{2,1,0:T(8,128)S(1)}) custom-call(f32[273,144,128]{2,1,0:T(8,128)S(1)} %get-tuple-element.18.acc), custom_call_target="tpu_custom_call" | custom-call | flops 4194304 | bytes 16777216 | tf_op jit(solution)/shard_map/fold/pallas_call | solution.py:433
  60.3 0.0 collective-permute-done.2.edge
  60.3 1.5 %edges.1 = f32[2,1024,1024]{2,1,0:T(8,128)} custom-call(f32[2,8,8,128]{3,2,1,0:T(8,128)S(1)} %collective-permute-done.2.edge, f32[2,1024,128]{2,1,0:T(8,128)S(1)} %get-tuple-element.19.first, f32[2,1024,1024]{2,1,0:T(8,128)} %get-tuple-element.20.grid_in), custom_call_target="tpu_custom_call", output_to_operand_aliasing={{}: (2, {})} | custom-call | tf_op jit(solution)/shard_map/edges/pallas_call | solution.py:446
  (1 shorter events, 0.0 us)
Async XLA Ops:
  23.3 17.4 %collective-permute-start.1 = (f32[588,1,128]{2,1,0:T(1,128)S(1)}, f32[588,1,128]{2,1,0:T(1,128)S(1)}, u32[]{:S(2)}, u32[]{:S(2)}) collective-permute-start(f32[588,1,128]{2,1,0:T(1,128)S(1)} %bitcast.6), channel_id=1, source_target_pairs={{0,16},{16,0},{1,17},{17,1},{2,18},{18,2},{3,19},{19,3},{4,20},{20... | collective-permute-start | bytes 903176 | tf_op jit(solution)/shard_map/ppermute | solution.py:389
  38.8 11.8 %collective-permute-start = (f32[196,1,128]{2,1,0:T(1,128)S(1)}, f32[196,1,128]{2,1,0:T(1,128)S(1)}, u32[]{:S(2)}, u32[]{:S(2)}) collective-permute-start(f32[196,1,128]{2,1,0:T(1,128)S(1)} %get-tuple-element.15), channel_id=1, source_target_pairs={{0,16},{16,0},{1,17},{17,1},{2,18},{18,2},{3,19},{19,3},{4,20},{20... | collective-permute-start | bytes 301064 | tf_op jit(solution)/shard_map/ppermute | solution.py:420
  55.8 4.5 %collective-permute-start.2 = (f32[2,8,8,128]{3,2,1,0:T(8,128)S(1)}, f32[2,8,8,128]{3,2,1,0:T(8,128)S(1)}, u32[]{:S(2)}, u32[]{:S(2)}) collective-permute-start(f32[2,8,8,128]{3,2,1,0:T(8,128)S(1)} %get-tuple-element.17), channel_id=1, source_target_pairs={{0,4},{4,8},{8,12},{12,16},{16,20},{20,24},{24,28},{1,5},{5,9},{9,... | collective-permute-start | bytes 196616 | tf_op jit(solution)/shard_map/ppermute | solution.py:346
